TPU v7x, 32 devices: a whole 2x2x4 slice. The times are simulated.
32 devices in a mesh: dp: 2 (over core), fsdp: 16 (over z, y, x).
Axes of the slice: x: 2, y: 2, z: 4, core: 2. Of those that a mesh axis runs over, the one named last changes fastest.
Arguments:
- tokens: bfloat16 [32768, 768], P(('dp', 'fsdp')), may hold values from -6 to 6
- cotangent: bfloat16 [32768, 768], P(('dp', 'fsdp')), may hold values from -6 to 6
- master_slots: float32 [18432, 768], P('fsdp'), as said below
- first_slots: float32 [18432, 768], P('fsdp')
- second_slots: float32 [18432, 768], P('fsdp')
- norm_gains: float32 [2, 768], replicated, may hold values from 0.5 to 1.5
- gains_first: float32 [2, 768], replicated, may hold values from -1086.116 to 1086.116
- gains_second: float32 [2, 768], replicated, may hold values from 10922 to 43690
- bias_table: float32 [32, 12], replicated, may hold values from -4 to 4
- table_first: float32 [32, 12], replicated, may hold values from -1086.116 to 1086.116
- table_second: float32 [32, 12], replicated, may hold values from 10922 to 43690
- bucket_ids: int32 [1023], replicated, may hold values from 0 to 31
- valid_len: int32 [64], P(('dp', 'fsdp')), may hold values from 128 to 512, as said below
- task_sizes: int32 [40], replicated, may hold values from 1 to 4, 64 in all
- owner_list: int32 [1152], replicated, may hold values from 0 to 15, as said below
Outputs:
- block_out: bfloat16 [32768, 768], P(('dp', 'fsdp'))
- grad_input: float32 [32768, 768], P(('dp', 'fsdp'))
- grad_slots: float32 [18432, 768], P('fsdp')
- grad_gains: float32 [2, 768], replicated
- grad_table: float32 [32, 12], replicated
- first_new: float32 [18432, 768], P('fsdp')
- second_new: float32 [18432, 768], P('fsdp')
- master_new: float32 [18432, 768], P('fsdp')
- master_copy: bfloat16 [18432, 768], P('fsdp')
- gains_first_new: float32 [2, 768], replicated
- gains_second_new: float32 [2, 768], replicated
- gains_new: float32 [2, 768], replicated
- table_first_new: float32 [32, 12], replicated
- table_second_new: float32 [32, 12], replicated
- table_new: float32 [32, 12], replicated
Inputs may be any that keep to these rules, and one draw needn't show every extreme that they name: `owner_list`: each block's owner along fsdp; no device owns more than 144 blocks, and one device owns exactly 144. Range r is blocks r * 72 to r * 72 + 71; no owner holds more than 9 blocks of one range, and some owner holds exactly 9 of some range. `valid_len`: some sequence is unpadded. `task_sizes`: they add up to 64. `bucket_ids`: entry j - i + 511 is the bucket of key j seen from query i. `master_slots`: unoccupied slots hold values too.
All inputs are finite; a program needn't handle non-finite values.
Results may differ from a plain program's by a relative error of at most 0.014.
The roundings to bfloat16 on the way count: a program that leaves them out, or rounds other values in their place, can miss the bound.
Values may be sent and summed in bfloat16 or wider, within the bound.
A program may use at most 320 MiB of HBM per device.

v0:
```python
import jax
import jax.numpy as jnp
from jax import lax
from jax.sharding import PartitionSpec as P

HEADS = 12
HEAD_DIM = 64
LEN = 512
BROWS = 8
OPT_STEP = 3


EPS_NORM = 1e-06
BETA_ONE = 0.5
BETA_TWO = 0.75
LEARN_RATE = 0.06
SMALL_RATE = 0.4
WEIGHT_DECAY = 0.01
EPS_ADAM = 1e-08
NEG_FILL = -1e30
HIGHEST = lax.Precision.HIGHEST


def product(left_side, right_side):
    return jnp.dot(left_side, right_side, preferred_element_type=jnp.float32)


def contract_rows(left_side, right_side):
    return lax.dot_general(
        left_side, right_side, (((0,), (0,)), ((), ())), preferred_element_type=jnp.float32
    )


def contract_cols(left_side, right_side):
    return lax.dot_general(
        left_side, right_side, (((1,), (1,)), ((), ())), preferred_element_type=jnp.float32
    )


def smooth_act(values):
    return jax.nn.gelu(values, approximate=True)


def slot_layout(owner_list, devices, capacity):
    block_count = owner_list.shape[0]
    onehot = (owner_list[:, None] == jnp.arange(devices, dtype=jnp.int32)[None, :]).astype(
        jnp.int32
    )
    rank_in = jnp.sum((jnp.cumsum(onehot, axis=0) - onehot) * onehot, axis=1)
    slot_of = owner_list * capacity + rank_in
    source = (
        jnp.zeros((devices * capacity,), jnp.int32)
        .at[slot_of]
        .set(jnp.arange(block_count, dtype=jnp.int32))
    )
    filled = (
        jnp.zeros((devices * capacity,), jnp.int32)
        .at[slot_of]
        .set(jnp.ones((block_count,), jnp.int32))
    )
    return (slot_of, source, filled, rank_in)


def split_rows(all_rows):
    model_width = all_rows.shape[1]
    hidden = (all_rows.shape[0] - 4 * model_width) // 2
    return (
        all_rows[:model_width],
        all_rows[model_width : 2 * model_width],
        all_rows[2 * model_width : 3 * model_width],
        all_rows[3 * model_width : 4 * model_width],
        all_rows[4 * model_width : 4 * model_width + hidden],
        all_rows[4 * model_width + hidden :],
    )


def norm_raw(values, gain_row):
    inv_rms = lax.rsqrt(jnp.mean(values * values, axis=-1, keepdims=True) + EPS_NORM)
    return values * inv_rms * gain_row


def expand_bias(bias_table, bucket_ids):
    length = (bucket_ids.shape[0] + 1) // 2
    onehot = jax.nn.one_hot(bucket_ids, bias_table.shape[0], dtype=jnp.float32)
    rel_rows = jnp.dot(onehot, bias_table, precision=HIGHEST)
    reverse = rel_rows[::-1].T
    tiled_rows = jnp.tile(reverse, (1, length + 1))[:, : 2 * length * length]
    return tiled_rows.reshape(reverse.shape[0], length, 2 * length)[:, :, :length][:, :, ::-1]


def masked_scores(seq_query, seq_key, rel_bias, length):
    scores = (
        jnp.einsum("qhd,khd->hqk", seq_query, seq_key, preferred_element_type=jnp.float32)
        + rel_bias
    )
    live = jnp.arange(seq_key.shape[0], dtype=jnp.int32)[None, None, :] < length
    return jnp.where(live, scores, NEG_FILL)


def adamw(weight, gradient, first_in, second, step_value, rate):
    first_out = BETA_ONE * first_in + (1.0 - BETA_ONE) * gradient
    second_out = BETA_TWO * second + (1.0 - BETA_TWO) * gradient * gradient
    fix_first = 1.0 - jnp.power(jnp.float32(BETA_ONE), step_value)
    fix_second = 1.0 - jnp.power(jnp.float32(BETA_TWO), step_value)
    update = first_out / fix_first / (jnp.sqrt(second_out / fix_second) + EPS_ADAM)
    return (first_out, second_out, weight - rate * (update + WEIGHT_DECAY * weight))


def body(
    tokens,
    cotangent,
    master_slots,
    first_slots,
    second_slots,
    norm_gains,
    gains_first,
    gains_second,
    bias_table,
    table_first,
    table_second,
    bucket_ids,
    valid_len,
    task_sizes,
    owner_list,
):
    devices = lax.axis_size("fsdp")
    replicas = lax.axis_size("dp")
    my_index = lax.axis_index("fsdp")
    capacity = master_slots.shape[0] // BROWS
    model_width = master_slots.shape[1]
    seq_dev = valid_len.shape[0]
    slot_of, source, filled, rank_in = slot_layout(owner_list, devices, capacity)
    sent_shard = master_slots.astype(jnp.bfloat16)

    def rebuild(gathered):
        blocks = gathered.reshape(devices * capacity, BROWS, model_width)[slot_of]
        return split_rows(blocks.reshape(-1, model_width))

    def by_seq(array_in):
        return array_in.reshape(seq_dev, LEN, HEADS, HEAD_DIM)

    def to_rows(array_in):
        return array_in.reshape(-1, model_width).astype(jnp.bfloat16)

    w_query, w_key, w_value, w_out, w_in, w_down = rebuild(
        lax.all_gather(sent_shard, "fsdp", axis=0, tiled=True)
    )
    rel_bias, bias_pull = jax.vjp(lambda table_in: expand_bias(table_in, bucket_ids), bias_table)
    inputs = tokens.astype(jnp.float32)
    hidden_one, norm_one_pull = jax.vjp(norm_raw, inputs, norm_gains[0])
    hidden_one = hidden_one.astype(jnp.bfloat16)
    queries = product(hidden_one, w_query).astype(jnp.bfloat16)
    keys_in = product(hidden_one, w_key).astype(jnp.bfloat16)
    values_in = product(hidden_one, w_value).astype(jnp.bfloat16)

    def attend_one(packed):
        seq_query, seq_key, seq_value, length = packed
        scores = masked_scores(seq_query, seq_key, rel_bias, length)
        row_max = jnp.max(scores, axis=-1, keepdims=True)
        exp_scores = jnp.exp(scores - row_max)
        totals = jnp.sum(exp_scores, axis=-1, keepdims=True)
        attn_probs = (exp_scores / totals).astype(jnp.bfloat16)
        context = jnp.einsum(
            "hqk,khd->qhd", attn_probs, seq_value, preferred_element_type=jnp.float32
        )
        return (context, row_max + jnp.log(totals))

    context, log_sums = lax.map(
        attend_one, (by_seq(queries), by_seq(keys_in), by_seq(values_in), valid_len)
    )
    context = to_rows(context)
    resid = inputs + product(context, w_out)
    hidden_two, norm_two_pull = jax.vjp(norm_raw, resid, norm_gains[1])
    hidden_two = hidden_two.astype(jnp.bfloat16)
    pre_act = contract_cols(hidden_two, w_in)
    active_full, act_pull = jax.vjp(smooth_act, pre_act)
    active = active_full.astype(jnp.bfloat16)
    block_out = (resid + product(active, w_down)).astype(jnp.bfloat16)
    first_seq = (lax.axis_index("dp") * devices + my_index) * seq_dev
    seq_ids = first_seq + jnp.arange(seq_dev, dtype=jnp.int32)
    task_ends = jnp.cumsum(task_sizes)
    task_count = task_sizes.shape[0]
    task_of = jnp.sum((task_ends[None, :] <= seq_ids[:, None]).astype(jnp.int32), axis=1)
    size_of = jnp.sum(
        jnp.where(
            task_of[:, None] == jnp.arange(task_count, dtype=jnp.int32)[None, :],
            task_sizes[None, :],
            0,
        ),
        axis=1,
    )
    seq_weight = jnp.float32(seq_dev * replicas * devices) / (
        jnp.float32(task_count) * size_of.astype(jnp.float32)
    )
    back_out = (
        cotangent.astype(jnp.float32).reshape(seq_dev, LEN, model_width) * seq_weight[:, None, None]
    ).reshape(-1, model_width)
    w_query, w_key, w_value, w_out, w_in, w_down = rebuild(
        lax.all_gather(sent_shard, "fsdp", axis=0, tiled=True)
    )
    down_back = back_out.astype(jnp.bfloat16)
    grad_down = contract_rows(active, down_back)
    act_back = contract_cols(down_back, w_down)
    (pre_full,) = act_pull(act_back)
    pre_back = pre_full.astype(jnp.bfloat16)
    grad_in = contract_rows(pre_back, hidden_two)
    resid_part, gain_two = norm_two_pull(product(pre_back, w_in))
    resid_back = back_out + resid_part
    out_back = resid_back.astype(jnp.bfloat16)
    grad_out = contract_rows(context, out_back)
    context_back = contract_cols(out_back, w_out).astype(jnp.bfloat16)

    def attend_back(score_sum, packed):
        seq_query, seq_key, seq_value, seq_back, length, log_sum = packed
        scores = masked_scores(seq_query, seq_key, rel_bias, length)
        attn_probs = jnp.exp(scores - log_sum)
        value_grad = jnp.einsum(
            "hqk,qhd->khd",
            attn_probs.astype(jnp.bfloat16),
            seq_back,
            preferred_element_type=jnp.float32,
        )
        prob_grad = jnp.einsum(
            "qhd,khd->hqk", seq_back, seq_value, preferred_element_type=jnp.float32
        )
        score_back = (
            attn_probs * (prob_grad - jnp.sum(attn_probs * prob_grad, axis=-1, keepdims=True))
        ).astype(jnp.bfloat16)
        query_grad = jnp.einsum(
            "hqk,khd->qhd", score_back, seq_key, preferred_element_type=jnp.float32
        )
        key_grad = jnp.einsum(
            "hqk,qhd->khd", score_back, seq_query, preferred_element_type=jnp.float32
        )
        return (score_sum + score_back.astype(jnp.float32), (query_grad, key_grad, value_grad))

    score_sum, (query_grad, key_grad, value_grad) = lax.scan(
        attend_back,
        jnp.zeros_like(rel_bias),
        (
            by_seq(queries),
            by_seq(keys_in),
            by_seq(values_in),
            by_seq(context_back),
            valid_len,
            log_sums,
        ),
    )
    query_back = to_rows(query_grad)
    key_back = to_rows(key_grad)
    value_back = to_rows(value_grad)
    grad_query = contract_rows(hidden_one, query_back)
    grad_key = contract_rows(hidden_one, key_back)
    grad_value = contract_rows(hidden_one, value_back)
    hidden_back = (
        contract_cols(query_back, w_query)
        + contract_cols(key_back, w_key)
        + contract_cols(value_back, w_value)
    )
    input_part, gain_one = norm_one_pull(hidden_back)
    grad_input = resid_back + input_part
    (table_grad,) = bias_pull(score_sum)
    grad_rows = jnp.concatenate(
        [grad_query, grad_key, grad_value, grad_out, grad_in, grad_down], axis=0
    )
    slotted = jnp.where(
        filled[:, None, None] > 0, grad_rows.reshape(-1, BROWS, model_width)[source], 0.0
    ).reshape(-1, model_width)
    owned_grads = lax.psum_scatter(slotted, "fsdp", scatter_dimension=0, tiled=True)
    grad_slots = lax.psum(owned_grads, "dp")
    grad_gains, grad_table = lax.psum((jnp.stack([gain_one, gain_two]), table_grad), ("dp", "fsdp"))
    step_value = jnp.float32(OPT_STEP)
    first_new, second_new, master_new = adamw(
        master_slots, grad_slots, first_slots, second_slots, step_value, LEARN_RATE
    )
    gains_first_new, gains_second_new, gains_new = adamw(
        norm_gains, grad_gains, gains_first, gains_second, step_value, SMALL_RATE
    )
    table_first_new, table_second_new, table_new = adamw(
        bias_table, grad_table, table_first, table_second, step_value, SMALL_RATE
    )
    return (
        block_out,
        grad_input,
        grad_slots,
        grad_gains,
        grad_table,
        first_new,
        second_new,
        master_new,
        master_new.astype(jnp.bfloat16),
        gains_first_new,
        gains_second_new,
        gains_new,
        table_first_new,
        table_second_new,
        table_new,
    )


def solution(mesh):
    in_specs = (
        P(("dp", "fsdp"), None),
        P(("dp", "fsdp"), None),
        P("fsdp", None),
        P("fsdp", None),
        P("fsdp", None),
        P(),
        P(),
        P(),
        P(),
        P(),
        P(),
        P(),
        P(("dp", "fsdp")),
        P(),
        P(),
    )
    out_specs = (
        P(("dp", "fsdp"), None),
        P(("dp", "fsdp"), None),
        P("fsdp", None),
        P(),
        P(),
        P("fsdp", None),
        P("fsdp", None),
        P("fsdp", None),
        P("fsdp", None),
        P(),
        P(),
        P(),
        P(),
        P(),
        P(),
    )
    return jax.shard_map(body, mesh=mesh, in_specs=in_specs, out_specs=out_specs, check_vma=False)
```

profile of v0, /device:TPU:0, one launch (start us, length us, event | category | flops | bytes accessed | tf_op | source)
XLA Modules:
  0.0 1769.8 jit_solution(4273857482241004045)
XLA Ops:
  13.2 4.6 reduce-window.18
  18.5 6.5 scatter_custom_fusion
  25.0 6.5 scatter_custom_fusion.1
  37.9 11.9 tile.4
  49.8 39.9 %tile.10 = f32[12,524799]{1,0:T(8,128)} reshape(f32[12,513,1023]{2,1,0:T(8,128)} %tile.4) | data formatting | bytes 50380704 | tf_op jit(solution)/shard_map/jvp()/tile | solution.py:87
  89.7 10.5 slice-done
  100.2 35.8 %copy.129 = f32[2,8,512,1024]{3,2,1,0:T(8,128)} copy(f32[2,8,512,1024]{3,1,2,0:T(8,128)S(1)} %bitcast.212) | data formatting | bytes 67108864
  136.1 10.6 slice.88
  146.7 101.1 %rev.13 = f32[12,512,512]{2,1,0:T(8,128)} reverse(f32[12,512,512]{2,1,0:T(8,128)} %slice.88), dimensions={2} | reverse | bytes 25165824 | tf_op jit(solution)/shard_map/jvp()/rev | solution.py:88
  247.7 12.6 copy.96
  261.9 53.5 %all-gather.2.cloned.1.call-done = bf16[18432,768]{1,0:T(8,128)(2,1)} async-done(((bf16[1152,768]{1,0:T(8,128)(2,1)}), bf16[18432,768]{1,0:T(8,128)(2,1)}) %all-gather.2.cloned.1.call-update) | async-done | bytes 28311568 | tf_op jit(solution)/shard_map/all_gather | solution.py:146
  315.4 17.0 gather_fusion
  335.3 4.0 convolution_convert_fusion.2
  339.3 4.0 convolution_convert_fusion.3
  364.5 25.2 %while.29 = (s32[]{:T(128)}, bf16[2,512,12,64]{1,3,2,0:T(8,128)(2,1)}, f32[2,12,512,1]{2,1,3,0:T(8,128)S(1)}, bf16[2,512,12,64]{1,3,2,0:T(8,128)(2,1)}, s32[2]{0...) while((s32[]{:T(128)}, ...), condition=%wide.region_7.8_spmd, body=%wide.region_4.7_spmd.sunk | while | flops 830466560 | bytes 60796052 | solution.py:168
  365.9 6.2 fusion.117
  378.4 6.2 fusion.117
  396.9 11.4 fusion.43
  408.3 20.9 %fusion.40 = (bf16[1024,3072]{1,0:T(8,128)(2,1)}, f32[1024,3072]{1,0:T(8,128)}) fusion(f32[1024,3072]{1,0:T(8,128)} %fusion.43, bf16[1152,8,768]{2,1,0:T(8,128)(2,1)} %gather_fusion, f32[1024,768]{0,1:T(8,128)S(1)} %get-tuple-element.338, f32[768]{0:T(1024)S(1)} %copy-done.38, f32[1024]{0:T(1024)S(1)} %fusion.76), kind=kOutput, calls=%fused_computation.60 | convolution fusion | flops 4897112064 | bytes 39328768 | tf_op jit(solution)/shard_map/dot_general | solution.py:35
  429.3 9.7 multiply_reduce_fusion.1
  441.5 3.9 convolution_convert_fusion
  448.0 4.2 reshape.230
  459.1 88.6 %while.30 = (s32[]{:T(128)}, f32[12,512,512]{1,2,0:T(8,128)}, bf16[2,512,12,64]{1,3,2,0:T(8,128)(2,1)}, bf16[2,512,12,64]{1,3,2,0:T(8,128)(2,1)}, bf16[2,512,12,...) while((s32[]{:T(128)}, f32[12,512,512]{1,2,0:T(8,128)}, ...), condition=%wide.region_15.16_spmd.clone, body=%wide.region_13.15_spmd.clone.sunk | while | flops 2051009024 | bytes 180222304 | solution.py:237
  464.1 10.5 multiply_reduce_fusion.5
  474.6 7.8 bitcast_dynamic-update-slice_fusion.14
  482.4 13.1 select_add_fusion.2
  495.4 4.2 bitcast_dynamic-update-slice_fusion.13
  506.9 10.5 multiply_reduce_fusion.5
  517.4 7.8 bitcast_dynamic-update-slice_fusion.14
  525.2 15.8 select_add_fusion.2
  541.0 4.2 bitcast_dynamic-update-slice_fusion.13
  568.2 8.1 convolution_dynamic-update-slice_fusion.1
  576.4 10.7 convolution_dynamic-update-slice_fusion
  587.1 56.3 %gather_fusion.1 = f32[2304,8,768]{2,1,0:T(8,128)} fusion(f32[1152,8,768]{2,1,0:T(8,128)} %bitcast.18, s32[3072]{0:T(1024)S(1)} %copy-done.29), kind=kCustom, calls=%fused_computation.1 | custom fusion | bytes 113255424 | tf_op jit(solution)/shard_map/gather | solution.py:267
  643.4 37.5 %bitcast_select_fusion = f32[18432,768]{1,0:T(8,128)} fusion(f32[2304,8,768]{2,1,0:T(8,128)} %gather_fusion.1, pred[18432]{0:T(1024)(128)(4,1)S(1)} %copy-done.28), kind=kLoop, calls=%fused_computation.51 | loop fusion | flops 14155776 | bytes 113264640 | tf_op jit(solution)/shard_map/jit(_where)/select_n | solution.py:266
  680.9 772.9 %reduce-scatter.2.cloned.1.call-done = f32[1152,768]{1,0:T(8,128)} async-done(((f32[18432,768]{1,0:T(8,128)}), f32[1152,768]{1,0:T(8,128)}) %reduce-scatter.2.cloned.1.call-update) | async-done | bytes 3538960 | tf_op jit(solution)/shard_map/reduce_scatter | solution.py:269
  1453.9 12.2 add_convert_fusion
  1485.6 95.9 %rev.14 = f32[12,512,512]{1,2,0:T(8,128)} reverse(f32[12,512,512]{1,2,0:T(8,128)} %get-tuple-element.128), dimensions={2} | reverse | bytes 25165824 | tf_op jit(solution)/shard_map/transpose(jvp())/rev | solution.py:88
  1581.5 12.6 copy.127
  1594.1 7.2 pad.6.clone
  1601.4 11.3 pad.12
  1612.6 28.3 %copy.135 = f32[2,8,512,1024]{3,1,2,0:T(8,128)S(1)} copy(f32[2,8,512,1024]{3,2,1,0:T(8,128)} %bitcast.214) | data formatting | bytes 67108864
  1640.9 11.2 pad.7
  1652.1 41.6 %reshape.235 = f32[12,513,1023]{2,1,0:T(8,128)} reshape(f32[12,524799]{1,0:T(8,128)} %pad.7) | data formatting | bytes 50380704 | tf_op jit(solution)/shard_map/transpose(jvp())/reshape | solution.py:87
  1693.7 9.9 reduce_sum.133
  1703.6 4.3 reverse.1
  1710.5 39.7 %all-reduce.2 = (f32[2,768]{1,0:T(2,128)}, f32[32,12]{0,1:T(8,128)}) all-reduce(f32[2,768]{1,0:T(2,128)S(1)} %pad_maximum_fusion, f32[32,12]{0,1:T(8,128)} %fusion.61), channel_id=1, replica_groups=mesh['dp'=2,'fsdp'=16] {'dp','fsdp'}, use_global_device_ids=true, to_apply=%region_23.24 | all-reduce | flops 1920 | bytes 15360 | tf_op jit(solution)/shard_map/psum | solution.py:271
  1752.9 8.3 fusion.87
  (232 shorter events, 132.0 us)
Async XLA Ops:
  7.2 3.6 copy-start.46
  7.2 4.9 copy-start.47
  7.2 4.9 copy-start.44
  7.2 6.0 copy-start.27
  7.2 308.2 %all-gather.2.cloned.1.call-start = ((), (), s32[]{:S(2)}) async-start(), calls=%async_computation.1 | async-start | bytes 30081024 | tf_op jit(solution)/shard_map/all_gather | solution.py:146
  10.7 23.2 %copy-start.21 = (bf16[1024,768]{1,0:T(8,128)(2,1)S(1)}, bf16[1024,768]{1,0:T(8,128)(2,1)}, u32[]{:S(2)}) copy-start(bf16[1024,768]{1,0:T(8,128)(2,1)} %param.19) | copy-start | bytes 4718596
  10.7 1443.2 %reduce-scatter.2.cloned.1.call-start = ((), (), s32[]{:S(2)}) async-start(), calls=%async_computation.2 | async-start | bytes 60162048 | tf_op jit(solution)/shard_map/reduce_scatter | solution.py:269
  34.7 304.6 %copy-start.4 = (bf16[1024,768]{0,1:T(8,128)(2,1)}, bf16[1024,768]{0,1:T(8,128)(2,1)S(1)}, u32[]{:S(2)}) copy-start(bf16[1024,768]{0,1:T(8,128)(2,1)S(1)} %copy.89) | copy-start | bytes 4718596
  89.7 10.5 slice-start
  247.7 13.2 copy-start.36
  261.6 77.7 %copy-start.30 = (f32[768]{0:T(1024)}, f32[768]{0:T(1024)S(1)}, u32[]{:S(2)}) copy-start(f32[768]{0:T(1024)S(1)} %get-tuple-element.278) | copy-start | bytes 9220
  261.9 70.6 %copy-start.34 = (f32[1024]{0:T(1024)}, f32[1024]{0:T(1024)S(1)}, u32[]{:S(2)}) copy-start(f32[1024]{0:T(1024)S(1)} %fusion.52) | copy-start | bytes 12292
  261.9 77.3 %copy-start.32 = (f32[1024]{0:T(1024)}, f32[1024]{0:T(1024)S(1)}, u32[]{:S(2)}) copy-start(f32[1024]{0:T(1024)S(1)} %fusion.75) | copy-start | bytes 12292
  360.3 4.2 copy-start.48
  389.7 3.6 copy-start.5
  393.3 3.6 copy-start.22
  393.3 3.6 copy-start.17
  393.3 3.6 copy-start.40
  396.8 42.1 %copy-start.19 = (f32[1024,768]{0,1:T(8,128)}, f32[1024,768]{0,1:T(8,128)S(1)}, u32[]{:S(2)}) copy-start(f32[1024,768]{0,1:T(8,128)S(1)} %get-tuple-element.338) | copy-start | bytes 9437188
  396.9 42.1 %copy-start.42 = (f32[1024]{0:T(1024)}, f32[1024]{0:T(1024)S(1)}, u32[]{:S(2)}) copy-start(f32[1024]{0:T(1024)S(1)} %fusion.76) | copy-start | bytes 12292
  396.9 11.4 copy-start.38
  495.4 4.2 copy-start.3
  495.4 4.2 copy-start.14
  541.0 4.2 copy-start.3
  541.0 4.2 copy-start.14
  547.6 3.6 copy-start.16
  555.4 2.9 copy-start.26
  561.2 2.9 copy-start.11
  561.2 2.9 copy-start.23
  561.2 5.8 slice-start.1
  564.1 2.9 copy-start.20
  564.1 2.9 copy-start.39
  564.2 2.9 copy-start.43
  564.2 4.0 slice-start.2
  564.2 12.2 slice-start.3
  568.2 8.1 copy-start.18
  568.2 8.1 copy-start.41
  568.2 8.1 slice-start.4
  568.2 8.2 slice-start.5
  576.4 10.7 copy-start.29
  587.1 56.3 %copy-start.28 = (pred[18432]{0:T(1024)(128)(4,1)S(1)}, pred[18432]{0:T(1024)(128)(4,1)}, u32[]{:S(2)}) copy-start(pred[18432]{0:T(1024)(128)(4,1)} %broadcast_in_dim.114) | copy-start | bytes 55300
  680.9 1072.0 %all-reduce.5.cloned.1.call-start = ((), (), s32[]{:S(2)}) async-start(), calls=%async_computation.3 | async-start | bytes 7077888 | tf_op jit(solution)/shard_map/psum | solution.py:270
  1469.3 3.3 copy-start.25
  1475.3 4.3 copy-start.35
  1475.3 4.3 copy-start.12
  1693.7 56.5 %copy-start.37 = (f32[2,768]{1,0:T(2,128)S(1)}, f32[2,768]{1,0:T(2,128)}, u32[]{:S(2)}) copy-start(f32[2,768]{1,0:T(2,128)} %param.24) | copy-start | bytes 18436
  1693.7 59.2 %copy-start.9 = (f32[1152,768]{1,0:T(8,128)S(1)}, f32[1152,768]{1,0:T(8,128)}, u32[]{:S(2)}) copy-start(f32[1152,768]{1,0:T(8,128)} %param.21) | copy-start | bytes 10616836
  1752.9 8.3 copy-start.8
  (17 other events, 31.6 us)
Sparse Core Ops, SparseCore 0:
  11.4 303.9 all-gather.1
  681.0 772.7 reduce-scatter.1
  1456.2 23.0 all-reduce.4
where the time goes:
time: 1790 us; the launch traced here: 1770 us
  waiting for transfers between devices  826 us (46%)
  local copies, waits for them, and re-layouts  594 us (33%)
  matrix products  187 us (10%)
  other arithmetic  107 us (6%)
  blocking collectives  39.7 us (2%)
    reduce_scatter x1, waiting for transfers between devices, body(): lax.psum_scatter(slotted, 'fsdp', scatter_dimension=0, tiled=True)  773 us
    rev x2, local copies, waits for them, and re-layouts, expand_bias(): tiled_rows.reshape(reverse.shape[0], length, 2 * length)[:, :, :length]  197 us
    unnamed x112, local copies, waits for them, and re-layouts  113 us
    gather x1, local copies, waits for them, and re-layouts, body(): grad_rows.reshape(-1, BROWS, model_width)[source]  56.3 us
    all_gather x1, waiting for transfers between devices, body(): lax.all_gather(sent_shard, 'fsdp', axis=0, tiled=True)  53.5 us
    another operation x2, local copies, waits for them, and re-layouts, expand_bias(): tiled_rows = jnp.tile(reverse, (1, length + 1))[:, :2 * length * length]  51.8 us
    dot_general x6, matrix products, contract_cols(): lax.dot_general(left_side, right_side, (((1,), (1,)), ((), ())), preferre...  45.9 us
    reshape x1, local copies, waits for them, and re-layouts, expand_bias(): tiled_rows = jnp.tile(reverse, (1, length + 1))[:, :2 * length * length]  41.6 us
  transfers between devices with their start and end apart: 3, of which 2 were waited for; matrix products, arithmetic and copies ran while one was open for 28% of the time, Pallas kernels for 0%

commit v1 on v0

--- a/solution.py
+++ b/solution.py
@@ -1,24 +1,1082 @@
+import functools
 import jax
 import jax.numpy as jnp
 from jax import lax
+from jax.experimental import pallas as pl
+from jax.experimental.pallas import tpu as pltpu
 from jax.sharding import PartitionSpec as P
 
 HEADS = 12
 HEAD_DIM = 64
 LEN = 512
 BROWS = 8
-OPT_STEP = 3
-
-
 EPS_NORM = 1e-06
+NEG_FILL = -1e30
+HIGHEST = lax.Precision.HIGHEST
+MESH = pl.DeviceIdType.MESH
+BF = jnp.bfloat16
+F32 = jnp.float32
+
+CHIPS = 16
+RANGE_BLOCKS = 72
+RANGE_ROWS = 576
+PAIR_ROWS = 80
+PACK_ROWS = CHIPS * PAIR_ROWS
+ROUNDS = 3
+TILE = 128
+HALF = 3 * TILE
+NT = (((1,), (1,)), ((), ()))
+NN = (((1,), (0,)), ((), ()))
+
+
+def dotf(a, b, dims=NN):
+    return lax.dot_general(a, b, dims, preferred_element_type=F32)
+
+
+def unit_place(v):
+    return v // 3, v % 3
+
+
+def unit_slice(v, core):
+    rng, til = unit_place(v)
+    return (
+        pl.ds(pl.multiple_of(rng * RANGE_ROWS, 64), RANGE_ROWS),
+        pl.ds(pl.multiple_of(core * HALF + til * TILE, TILE), TILE),
+    )
+
+
+def half_slice(v, core, half):
+    rng, til = unit_place(v)
+    return (
+        pl.ds(pl.multiple_of(rng * RANGE_ROWS + half * (RANGE_ROWS // 2), 32), RANGE_ROWS // 2),
+        pl.ds(pl.multiple_of(core * HALF + til * TILE, TILE), TILE),
+    )
+
+
+def place():
+    core = lax.axis_index("dp")
+    chip = lax.axis_index("fsdp")
+    xpos = chip % 2
+    ypos = (chip // 2) % 2
+    zpos = chip // 4
+    xnbr = chip + 1 - 2 * xpos
+    ynbr = chip + 2 - 4 * ypos
+    return core, chip, xpos, ypos, zpos, xnbr, ynbr
+
+
+def enter(core, chip):
+    barrier = pltpu.get_barrier_semaphore()
+    for step in range(1, CHIPS):
+        pl.semaphore_signal(
+            barrier, inc=1, device_id=(core, lax.rem(chip + step, CHIPS)), device_id_type=MESH
+        )
+    pl.semaphore_signal(barrier, inc=1, device_id=(1 - core, chip), device_id_type=MESH)
+    pl.semaphore_wait(barrier, CHIPS)
+
+
+def gather_kernel(
+    master_ref, idx_pack_ref, idx_unit_ref, tokens_ref, gains_ref, rel_ref, len_ref,
+    w_hbm, q_ref, k_ref, v_ref, ctx_ref, p_hbm,
+    weights, sendbuf, recvbuf, hidden, base, s_scr, p_scr,
+    a2a_send, a2a_recv, z_send, z_recv, x_send, x_recv, y_send, y_recv,
+    da_send, da_recv, db_send, db_recv, s_send, s_recv, w_sem, p_sem,
+):
+    core, chip, xpos, ypos, zpos, xnbr, ynbr = place()
+    col = ypos * 2 + xpos
+    xcol = ypos * 2 + (1 - xpos)
+    ycol = (1 - ypos) * 2 + xpos
+    dcol = (1 - ypos) * 2 + (1 - xpos)
+
+    def remote(src, dst, ssem, rsem, device):
+        return pltpu.make_async_remote_copy(
+            src_ref=src, dst_ref=dst, send_sem=ssem, recv_sem=rsem, device_id=device, device_id_type=MESH
+        )
+
+    for part in range(4):
+        rows = PACK_ROWS // 4
+        onehot = (
+            lax.broadcasted_iota(jnp.int32, (rows, master_ref.shape[0]), 1)
+            == idx_pack_ref[part * rows : (part + 1) * rows, :]
+        ).astype(F32).astype(BF)
+        own_half = master_ref[:, pl.ds(pl.multiple_of(core * HALF, TILE), HALF)].astype(BF)
+        packed = dotf(onehot, own_half).astype(BF)
+        for til in range(3):
+            sendbuf[til, part * rows : (part + 1) * rows, :] = packed[:, til * TILE : (til + 1) * TILE]
+
+    enter(core, chip)
+
+    def a2a_copy(rnd, step):
+        dest = lax.rem(chip + step, CHIPS)
+        rng, til = unit_place(rnd * CHIPS + dest)
+        return remote(
+            sendbuf.at[til, pl.ds(pl.multiple_of(rng * PAIR_ROWS, 16), PAIR_ROWS), :],
+            recvbuf.at[rnd, pl.ds(pl.multiple_of(chip * PAIR_ROWS, 16), PAIR_ROWS), :],
+            a2a_send.at[rnd, step], a2a_recv.at[rnd, step], (core, dest),
+        )
+
+    for rnd in range(ROUNDS):
+        for step in range(1, CHIPS):
+            a2a_copy(rnd, step).start()
+        rng, til = unit_place(rnd * CHIPS + chip)
+        recvbuf[rnd, pl.ds(pl.multiple_of(chip * PAIR_ROWS, 16), PAIR_ROWS), :] = sendbuf[
+            til, pl.ds(pl.multiple_of(rng * PAIR_ROWS, 16), PAIR_ROWS), :
+        ]
+
+    for part in range(tokens_ref.shape[0] // 128):
+        rows = slice(part * 128, (part + 1) * 128)
+        values = tokens_ref[rows, :].astype(F32)
+        inv_rms = lax.rsqrt(jnp.mean(values * values, axis=-1, keepdims=True) + EPS_NORM)
+        hidden[rows, :] = (values * inv_rms * gains_ref[0:1, :]).astype(BF)
+
+    def bands(h, _):
+        wide = jnp.broadcast_to(rel_ref[pl.ds(h, 1), :], (128, 1024))
+        base[pl.ds(h, 1)] = pltpu.roll(wide, 0, 1, stride=1, stride_axis=0)[:, :896][None]
+        return 0
+
+    lax.fori_loop(0, HEADS, bands, 0)
+
+    def own_unit(rnd):
+        for step in range(1, CHIPS):
+            a2a_copy(rnd, step).wait_recv()
+        v = rnd * CHIPS + chip
+        for part in range(2):
+            rows = RANGE_ROWS // 2
+            onehot = (
+                lax.broadcasted_iota(jnp.int32, (rows, PACK_ROWS), 1)
+                == idx_unit_ref[rnd, part * rows : (part + 1) * rows, :]
+            ).astype(F32).astype(BF)
+            weights[half_slice(v, core, part)] = dotf(onehot, recvbuf[rnd]).astype(BF)
+
+    def z_copy(rnd, off):
+        v = rnd * CHIPS + chip
+        dest = lax.rem(zpos + off, 4) * 4 + col
+        place_at = unit_slice(v, core)
+        return remote(
+            weights.at[place_at], weights.at[place_at],
+            z_send.at[rnd, off], z_recv.at[rnd, off], (core, dest),
+        )
+
+    def plane(off):
+        return lax.rem(zpos + 4 - off, 4)
+
+    def unit_at(rnd, off, column):
+        return rnd * CHIPS + plane(off) * 4 + column
+
+    def x_copy(rnd, off):
+        at = unit_slice(unit_at(rnd, off, col), core)
+        return remote(weights.at[at], weights.at[at], x_send.at[rnd, off], x_recv.at[rnd, off], (core, xnbr))
+
+    def y_copy(rnd, off):
+        at = unit_slice(unit_at(rnd, off, col), core)
+        return remote(weights.at[at], weights.at[at], y_send.at[rnd, off], y_recv.at[rnd, off], (core, ynbr))
+
+    def da_copy(rnd, off):
+        at = half_slice(unit_at(rnd, off, xcol), core, 0)
+        return remote(weights.at[at], weights.at[at], da_send.at[rnd, off], da_recv.at[rnd, off], (core, ynbr))
+
+    def db_copy(rnd, off):
+        at = half_slice(unit_at(rnd, off, ycol), core, 1)
+        return remote(weights.at[at], weights.at[at], db_send.at[rnd, off], db_recv.at[rnd, off], (core, xnbr))
+
+    def s_copy(rnd, off, kind):
+        at = unit_slice(unit_at(rnd, off, (col, xcol, ycol, dcol)[kind]), core)
+        return remote(
+            weights.at[at], weights.at[at], s_send.at[kind, rnd, off], s_recv.at[kind, rnd, off], (1 - core, chip)
+        )
+
+    def z_start(rnd):
+        for off in (1, 2, 3):
+            z_copy(rnd, off).start()
+
+    def stage_a(rnd, off):
+        x_copy(rnd, off).start()
+        y_copy(rnd, off).start()
+        s_copy(rnd, off, 0).start()
+
+    def stage_b(rnd, off):
+        x_copy(rnd, off).wait_recv()
+        da_copy(rnd, off).start()
+        s_copy(rnd, off, 1).start()
+        y_copy(rnd, off).wait_recv()
+        db_copy(rnd, off).start()
+        s_copy(rnd, off, 2).start()
+
+    def stage_c(rnd, off):
+        da_copy(rnd, off).wait_recv()
+        db_copy(rnd, off).wait_recv()
+        s_copy(rnd, off, 3).start()
+
+    def z_wait(rnd, off):
+        z_copy(rnd, off).wait_recv()
+
+    def s_wait(rnd):
+        for off in range(4):
+            for kind in range(4):
+                s_copy(rnd, off, kind).wait_recv()
+
+    own_unit(0)
+    z_start(0)
+    stage_a(0, 0)
+    for rnd in (1, 2):
+        own_unit(rnd)
+        z_start(rnd)
+    z_wait(0, 1)
+    stage_a(0, 1)
+    stage_b(0, 0)
+    z_wait(0, 2)
+    stage_a(0, 2)
+    stage_b(0, 1)
+    stage_c(0, 0)
+    z_wait(0, 3)
+    stage_a(0, 3)
+    stage_a(1, 0)
+    stage_b(0, 2)
+    stage_c(0, 1)
+    z_wait(1, 1)
+    stage_a(1, 1)
+    stage_b(0, 3)
+    stage_c(0, 2)
+    stage_b(1, 0)
+    stage_c(0, 3)
+    s_wait(0)
+
+    model = hidden.shape[1]
+    for mat, out_ref in enumerate((q_ref, k_ref, v_ref)):
+        for til in range(model // 256):
+            cols = slice(til * 256, (til + 1) * 256)
+            out_ref[:, cols] = dotf(hidden[...], weights[mat * model : (mat + 1) * model, cols]).astype(BF)
+
+    row_id = lax.broadcasted_iota(jnp.int32, (128, LEN), 0)
+    lane_head = lax.broadcasted_iota(jnp.int32, (LEN, 128), 1) // HEAD_DIM
+
+    def p_copy(step, head):
+        seq, pair = step // 6, step % 6
+        return pltpu.make_async_copy(
+            p_scr.at[step % 2, head], p_hbm.at[seq * HEADS + pair * 2 + head], p_sem.at[step % 2, head]
+        )
+
+    def attend(step, _):
+        seq, pair = step // 6, step % 6
+        rows = pl.ds(pl.multiple_of(seq * LEN, LEN), LEN)
+        lanes = pl.ds(pl.multiple_of(pair * 128, 128), 128)
+        length = len_ref[seq]
+
+        @pl.when(step >= 2)
+        def _():
+            for head in range(2):
+                p_copy(step - 2, head).wait()
+
+        q_two = q_ref[rows, lanes]
+        k_two = k_ref[rows, lanes]
+        v_two = v_ref[rows, lanes].T
+        outs = []
+        for head in range(2):
+            k_one = jnp.where(lane_head == head, k_two, jnp.zeros_like(k_two))
+            top = jnp.full((8, LEN), NEG_FILL, F32)
+            for blk in range(4):
+                score = dotf(k_one[blk * 128 : (blk + 1) * 128], q_two, NT)
+                score = score + base[pair * 2 + head, :, 384 - 128 * blk : 896 - 128 * blk]
+                score = jnp.where(row_id + blk * 128 < length, score, NEG_FILL)
+                s_scr[head, blk * 128 : (blk + 1) * 128, :] = score
+                top = jnp.maximum(top, jnp.max(score.reshape(16, 8, LEN), axis=0))
+            top = jnp.max(top, axis=0, keepdims=True)
+            total = jnp.zeros((8, LEN), F32)
+            for blk in range(4):
+                part = jnp.exp(s_scr[head, blk * 128 : (blk + 1) * 128, :] - top)
+                s_scr[head, blk * 128 : (blk + 1) * 128, :] = part
+                total = total + jnp.sum(part.reshape(16, 8, LEN), axis=0)
+            inverse = 1.0 / jnp.sum(total, axis=0, keepdims=True)
+            for blk in range(4):
+                p_scr[step % 2, head, blk * 128 : (blk + 1) * 128, :] = (
+                    s_scr[head, blk * 128 : (blk + 1) * 128, :] * inverse
+                ).astype(BF)
+            outs.append(dotf(v_two[head * HEAD_DIM : (head + 1) * HEAD_DIM], p_scr[step % 2, head]))
+            p_copy(step, head).start()
+        ctx_ref[rows, lanes] = jnp.concatenate(outs, axis=0).T.astype(BF)
+        return 0
+
+    def w_copy(rnd):
+        at = slice(rnd * 3072, (rnd + 1) * 3072)
+        return pltpu.make_async_copy(weights.at[at], w_hbm.at[at], w_sem.at[rnd])
+
+    lax.fori_loop(0, 4, attend, 0)
+    z_wait(1, 2)
+    stage_a(1, 2)
+    stage_b(1, 1)
+    stage_c(1, 0)
+    z_wait(1, 3)
+    stage_a(1, 3)
+    stage_a(2, 0)
+    stage_b(1, 2)
+    stage_c(1, 1)
+    lax.fori_loop(4, 8, attend, 0)
+    z_wait(2, 1)
+    stage_a(2, 1)
+    stage_b(1, 3)
+    stage_c(1, 2)
+    stage_b(2, 0)
+    stage_c(1, 3)
+    z_wait(2, 2)
+    stage_a(2, 2)
+    lax.fori_loop(8, 12, attend, 0)
+    stage_b(2, 1)
+    stage_c(2, 0)
+    z_wait(2, 3)
+    stage_a(2, 3)
+    stage_b(2, 2)
+    stage_c(2, 1)
+    stage_b(2, 3)
+    stage_c(2, 2)
+    stage_c(2, 3)
+    s_wait(1)
+    s_wait(2)
+    for rnd in range(ROUNDS):
+        w_copy(rnd).start()
+    for step in (10, 11):
+        for head in range(2):
+            p_copy(step, head).wait()
+    for rnd in range(ROUNDS):
+        w_copy(rnd).wait()
+        for step in range(1, CHIPS):
+            a2a_copy(rnd, step).wait_send()
+        for off in (1, 2, 3):
+            z_copy(rnd, off).wait_send()
+        for off in range(4):
+            x_copy(rnd, off).wait_send()
+            y_copy(rnd, off).wait_send()
+            da_copy(rnd, off).wait_send()
+            db_copy(rnd, off).wait_send()
+            for kind in range(4):
+                s_copy(rnd, off, kind).wait_send()
+
+
+VM = pl.BlockSpec(memory_space=pltpu.VMEM)
+SM = pl.BlockSpec(memory_space=pltpu.SMEM)
+ANY = pl.BlockSpec(memory_space=pl.ANY)
+
+
+def gather_forward(master, idx_pack, idx_unit, tokens, gains, rel, lens):
+    ntok, model = tokens.shape
+    rows = 4 * model + 2 * 3072
+    dma = pltpu.SemaphoreType.DMA
+    return pl.pallas_call(
+        gather_kernel,
+        name="gather_forward",
+        out_shape=(
+            jax.ShapeDtypeStruct((rows, model), BF),
+            jax.ShapeDtypeStruct((ntok, model), BF),
+            jax.ShapeDtypeStruct((ntok, model), BF),
+            jax.ShapeDtypeStruct((ntok, model), BF),
+            jax.ShapeDtypeStruct((ntok, model), BF),
+            jax.ShapeDtypeStruct((2 * HEADS, LEN, LEN), BF),
+        ),
+        in_specs=[VM, VM, VM, VM, VM, VM, SM],
+        out_specs=(ANY, VM, VM, VM, VM, ANY),
+        scratch_shapes=[
+            pltpu.VMEM((rows, model), BF),
+            pltpu.VMEM((3, PACK_ROWS, TILE), BF),
+            pltpu.VMEM((ROUNDS, PACK_ROWS, TILE), BF),
+            pltpu.VMEM((ntok, model), BF),
+            pltpu.VMEM((HEADS, 128, 896), F32),
+            pltpu.VMEM((2, LEN, LEN), F32),
+            pltpu.VMEM((2, 2, LEN, LEN), BF),
+            dma((ROUNDS, CHIPS)), dma((ROUNDS, CHIPS)),
+            dma((ROUNDS, 4)), dma((ROUNDS, 4)),
+            dma((ROUNDS, 4)), dma((ROUNDS, 4)),
+            dma((ROUNDS, 4)), dma((ROUNDS, 4)),
+            dma((ROUNDS, 4)), dma((ROUNDS, 4)),
+            dma((ROUNDS, 4)), dma((ROUNDS, 4)),
+            dma((4, ROUNDS, 4)), dma((4, ROUNDS, 4)),
+            dma((ROUNDS,)), dma((2, 2)),
+        ],
+        compiler_params=pltpu.CompilerParams(
+            collective_id=0, has_side_effects=True, vmem_limit_bytes=60 * 2**20
+        ),
+    )(master, idx_pack, idx_unit, tokens, gains, rel, lens)
+
+
+def slot_tables(owner_list, chip):
+    owners = owner_list.reshape(CHIPS, RANGE_BLOCKS)
+    counts = jnp.sum((owners == chip).astype(jnp.int32), axis=1)
+    tri = jnp.arange(CHIPS)[:, None] > jnp.arange(CHIPS)[None, :]
+    starts = jnp.sum(jnp.where(tri, counts[None, :], 0), axis=1)
+    blk = jnp.arange(PAIR_ROWS // BROWS, dtype=jnp.int32)[None, :, None]
+    sub = jnp.arange(BROWS, dtype=jnp.int32)[None, None, :]
+    pack = jnp.where(
+        blk < counts[:, None, None], (starts[:, None, None] + blk) * BROWS + sub, -1
+    ).reshape(PACK_ROWS)
+    v = jnp.arange(ROUNDS, dtype=jnp.int32) * CHIPS + chip
+    rng, _ = unit_place(v)
+    mine = jnp.stack([lax.dynamic_slice(owners, (rng[i], 0), (1, RANGE_BLOCKS))[0] for i in range(ROUNDS)])
+    before = jnp.arange(RANGE_BLOCKS)[:, None] > jnp.arange(RANGE_BLOCKS)[None, :]
+    rank = jnp.sum(
+        ((mine[:, :, None] == mine[:, None, :]) & before[None]).astype(jnp.int32), axis=2
+    )
+    unit = (
+        (mine * PAIR_ROWS + rank * BROWS)[:, :, None] + jnp.arange(BROWS, dtype=jnp.int32)[None, None, :]
+    ).reshape(ROUNDS, RANGE_ROWS)
+    return pack, unit
+
+
+def rel_values(bias_table, bucket_ids):
+    length = (bucket_ids.shape[0] + 1) // 2
+    onehot = jax.nn.one_hot(bucket_ids, bias_table.shape[0], dtype=F32)
+    rel = jnp.dot(onehot, bias_table, precision=HIGHEST)[::-1].T
+    rel = jnp.concatenate([rel, jnp.zeros((HEADS, 1), F32)], axis=1)
+    rel = jnp.concatenate([rel[:, 127:], rel[:, :127]], axis=1)
+    return jnp.concatenate([rel, jnp.zeros((4, 2 * length), F32)], axis=0)
+
+
+FF_CHUNK = 512
+GELU_A = 0.7978845608028654
+GELU_B = 0.044715 * GELU_A
+
+
+def gelu_pair(v):
+    sq = v * v
+    half = 0.5 + 0.5 * jnp.tanh(v * (GELU_A + GELU_B * sq))
+    act = v * half
+    return act, half + act * (1.0 - half) * (2.0 * GELU_A + 6.0 * GELU_B * sq)
+
+
+TN = (((0,), (0,)), ((), ()))
+
+
+def ffn_kernel(
+    tokens_ref, cot_ref, ctx_ref, gains_ref, weight_ref, w_hbm,
+    out_ref, rb_ref, cb_ref, gain_ref, grad_hbm,
+    weights, hidden, down, resid, out_acc, u_acc, act_s, pb_s, gbuf, w_sem, g_sem,
+):
+    ntok, model = tokens_ref.shape
+    hid = (weights.shape[0] - 4 * model) // 2
+    nchunk = hid // FF_CHUNK
+    first_in, first_down = 4 * model, 4 * model + hid
+    seq_len = LEN
+
+    def w_copy(start, rows, sem):
+        at = pl.ds(start, rows)
+        return pltpu.make_async_copy(w_hbm.at[at], weights.at[at], sem)
+
+    w_copy(3 * model, model, w_sem.at[0]).start()
+    for c in range(nchunk):
+        w_copy(first_in + c * FF_CHUNK, FF_CHUNK, w_sem.at[1 + c]).start()
+        w_copy(first_down + c * FF_CHUNK, FF_CHUNK, w_sem.at[1 + nchunk + c]).start()
+    w_copy(3 * model, model, w_sem.at[0]).wait()
+
+    tile = 256
+    ntile = ntok // tile
+
+    def head(i, _):
+        rows = pl.ds(pl.multiple_of(i * tile, tile), tile)
+        value = tokens_ref[rows, :].astype(F32) + dotf(
+            ctx_ref[rows, :], weights[3 * model : 4 * model, :]
+        )
+        resid[rows, :] = value
+        inv_rms = lax.rsqrt(jnp.mean(value * value, axis=-1, keepdims=True) + EPS_NORM)
+        hidden[rows, :] = (value * inv_rms * gains_ref[1:2, :]).astype(BF)
+        down[rows, :] = (cot_ref[rows, :].astype(F32) * weight_ref[i * tile // seq_len]).astype(BF)
+        out_acc[rows, :] = jnp.zeros((tile, model), F32)
+        u_acc[rows, :] = jnp.zeros((tile, model), F32)
+        return 0
+
+    lax.fori_loop(0, ntile, head, 0)
+
+    def g_copy(c, which):
+        start = (first_in, first_down)[which] + c * FF_CHUNK
+        return pltpu.make_async_copy(
+            gbuf.at[c % 2, which], grad_hbm.at[pl.ds(pl.multiple_of(start, FF_CHUNK), FF_CHUNK)],
+            g_sem.at[c % 2, which],
+        )
+
+    def chunk(c, _):
+        rows_in = pl.ds(pl.multiple_of(first_in + c * FF_CHUNK, FF_CHUNK), FF_CHUNK)
+        rows_down = pl.ds(pl.multiple_of(first_down + c * FF_CHUNK, FF_CHUNK), FF_CHUNK)
+        pltpu.make_async_copy(w_hbm.at[rows_in], weights.at[rows_in], w_sem.at[1 + c]).wait()
+        pltpu.make_async_copy(w_hbm.at[rows_down], weights.at[rows_down], w_sem.at[1 + nchunk + c]).wait()
+        for i in range(ntile):
+            rows = slice(i * tile, (i + 1) * tile)
+            pre = dotf(hidden[rows, :], weights[rows_in, :], NT)
+            back = dotf(down[rows, :], weights[rows_down, :], NT)
+            act, slope = gelu_pair(pre)
+            act = act.astype(BF)
+            pre_back = (back * slope).astype(BF)
+            act_s[rows, :] = act
+            pb_s[rows, :] = pre_back
+            out_acc[rows, :] += dotf(act, weights[rows_down, :])
+            u_acc[rows, :] += dotf(pre_back, weights[rows_in, :])
+
+        @pl.when(c >= 2)
+        def _():
+            g_copy(c - 2, 0).wait()
+            g_copy(c - 2, 1).wait()
+
+        gbuf[c % 2, 1] = dotf(act_s[...], down[...], TN).astype(BF)
+        g_copy(c, 1).start()
+        gbuf[c % 2, 0] = dotf(pb_s[...], hidden[...], TN).astype(BF)
+        g_copy(c, 0).start()
+        return 0
+
+    lax.fori_loop(0, nchunk, chunk, 0)
+
+    def tail(i, gain):
+        rows = pl.ds(pl.multiple_of(i * tile, tile), tile)
+        value = resid[rows, :]
+        out_ref[rows, :] = (value + out_acc[rows, :]).astype(BF)
+        inv_rms = lax.rsqrt(jnp.mean(value * value, axis=-1, keepdims=True) + EPS_NORM)
+        u = u_acc[rows, :]
+        gu = u * gains_ref[1:2, :]
+        normal = value * inv_rms
+        mean = jnp.mean(gu * normal, axis=-1, keepdims=True)
+        back = cot_ref[rows, :].astype(F32) * weight_ref[i * tile // seq_len] + inv_rms * (gu - normal * mean)
+        rb_ref[rows, :] = back
+        low = back.astype(BF)
+        hidden[rows, :] = low
+        cb_ref[rows, :] = dotf(low, weights[3 * model : 4 * model, :], NT).astype(BF)
+        return gain + jnp.sum((u * normal).reshape(tile // 8, 8, model), axis=0)
+
+    gain = lax.fori_loop(0, ntile, tail, jnp.zeros((8, model), F32))
+    gain_ref[...] = gain
+    for c in (nchunk - 2, nchunk - 1):
+        g_copy(c, 0).wait()
+        g_copy(c, 1).wait()
+    for part in range(2):
+        cols = slice(part * model // 2, (part + 1) * model // 2)
+        gbuf[part, 0, : model // 2, :] = dotf(ctx_ref[:, cols], hidden[...], TN).astype(BF)
+        pltpu.make_async_copy(
+            gbuf.at[part, 0, pl.ds(0, model // 2)],
+            grad_hbm.at[pl.ds(3 * model + part * model // 2, model // 2)], g_sem.at[part, 0],
+        ).start()
+    for part in range(2):
+        pltpu.make_async_copy(
+            gbuf.at[part, 0, pl.ds(0, model // 2)],
+            grad_hbm.at[pl.ds(3 * model + part * model // 2, model // 2)], g_sem.at[part, 0],
+        ).wait()
+
+
+def ffn_pass(tokens, cot, ctx, gains, seq_weight, w_all):
+    ntok, model = tokens.shape
+    rows = w_all.shape[0]
+    nchunk = (rows - 4 * model) // 2 // FF_CHUNK
+    dma = pltpu.SemaphoreType.DMA
+    return pl.pallas_call(
+        ffn_kernel,
+        name="ffn_pass",
+        out_shape=(
+            jax.ShapeDtypeStruct((ntok, model), BF),
+            jax.ShapeDtypeStruct((ntok, model), F32),
+            jax.ShapeDtypeStruct((ntok, model), BF),
+            jax.ShapeDtypeStruct((8, model), F32),
+            jax.ShapeDtypeStruct((rows, model), BF),
+        ),
+        in_specs=[VM, VM, VM, VM, SM, ANY],
+        out_specs=(VM, VM, VM, VM, ANY),
+        scratch_shapes=[
+            pltpu.VMEM((rows, model), BF),
+            pltpu.VMEM((ntok, model), BF),
+            pltpu.VMEM((ntok, model), BF),
+            pltpu.VMEM((ntok, model), F32),
+            pltpu.VMEM((ntok, model), F32),
+            pltpu.VMEM((ntok, model), F32),
+            pltpu.VMEM((ntok, FF_CHUNK), BF),
+            pltpu.VMEM((ntok, FF_CHUNK), BF),
+            pltpu.VMEM((2, 2, FF_CHUNK, model), BF),
+            dma((1 + 2 * nchunk,)), dma((2, 2)),
+        ],
+        compiler_params=pltpu.CompilerParams(vmem_limit_bytes=60 * 2**20),
+    )(tokens, cot, ctx, gains, seq_weight, w_all)
+
+
+def reduce_kernel(
+    tokens_ref, gains_ref, q_ref, k_ref, v_ref, ctx_ref, cb_ref, bucket_ref, gain_two_ref, idx_unit_ref,
+    rb_hbm, w_hbm, p_hbm, grad_hbm,
+    gin_ref, slot_ref, small_ref,
+    weights, gown, gsend, sib, xin, yin, dain, dbin, zin, expand,
+    hid_t, dq, dk, dv, diag, drow, p_scr, ds_scr, small,
+    w_sem, l_sem, p_sem, r_sem, h_send, h_recv, da_send, da_recv, db_send, db_recv,
+    x_send, x_recv, y_send, y_recv, z_send, z_recv, a2a_send, a2a_recv, half_send, half_recv,
+    sm_send, sm_recv,
+):
+    core, chip, xpos, ypos, zpos, xnbr, ynbr = place()
+    ntok, model = tokens_ref.shape
+    col = ypos * 2 + xpos
+    xcol = ypos * 2 + (1 - xpos)
+    ycol = (1 - ypos) * 2 + xpos
+    dcol = (1 - ypos) * 2 + (1 - xpos)
+    other = 1 - core
+    own_cols = pl.ds(pl.multiple_of(core * HALF, TILE), HALF)
+    other_cols = pl.ds(pl.multiple_of(other * HALF, TILE), HALF)
+    qkv_rows = 3 * model
+    nrange = gown.shape[0] // RANGE_ROWS
+    qkv_ranges = qkv_rows // RANGE_ROWS
+
+    def remote(src, dst, ssem, rsem, device):
+        return pltpu.make_async_remote_copy(
+            src_ref=src, dst_ref=dst, send_sem=ssem, recv_sem=rsem, device_id=device, device_id_type=MESH
+        )
+
+    def range_rows(rng):
+        return pl.ds(pl.multiple_of(rng * RANGE_ROWS, 64), RANGE_ROWS)
+
+    def load_copy(rng):
+        return pltpu.make_async_copy(
+            grad_hbm.at[range_rows(rng), own_cols], gown.at[range_rows(rng)], l_sem.at[rng]
+        )
+
+    def sib_copy(rng):
+        src = grad_hbm.at[range_rows(rng), other_cols] if rng >= qkv_ranges else gsend.at[range_rows(rng)]
+        return remote(src, sib.at[range_rows(rng)], h_send.at[rng], h_recv.at[rng], (other, chip))
+
+    def sib_wait(rng):
+        remote(
+            gown.at[range_rows(rng)], sib.at[range_rows(rng)], h_send.at[rng], h_recv.at[rng], (other, chip)
+        ).wait_recv()
+
+    w_all = pltpu.make_async_copy(w_hbm.at[pl.ds(0, qkv_rows)], weights, w_sem)
+    w_all.start()
+    enter(core, chip)
+    for rng in reversed(range(qkv_ranges, nrange)):
+        load_copy(rng).start()
+        sib_copy(rng).start()
+
+    def gslice(v):
+        rng, til = unit_place(v)
+        return (range_rows(rng), pl.ds(pl.multiple_of(til * TILE, TILE), TILE))
+
+    def ghalf(v, half):
+        rng, til = unit_place(v)
+        return (
+            pl.ds(pl.multiple_of(rng * RANGE_ROWS + half * (RANGE_ROWS // 2), 32), RANGE_ROWS // 2),
+            pl.ds(pl.multiple_of(til * TILE, TILE), TILE),
+        )
+
+    def plane(off):
+        return lax.rem(zpos + off, 4)
+
+    def unit_at(rnd, off, column):
+        return rnd * CHIPS + plane(off) * 4 + column
+
+    def da_copy(rnd, off):
+        at = ghalf(unit_at(rnd, off, dcol), 0)
+        return remote(gown.at[at], dain.at[rnd, off], da_send.at[rnd, off], da_recv.at[rnd, off], (core, ynbr))
+
+    def db_copy(rnd, off):
+        at = ghalf(unit_at(rnd, off, dcol), 1)
+        return remote(gown.at[at], dbin.at[rnd, off], db_send.at[rnd, off], db_recv.at[rnd, off], (core, xnbr))
+
+    def x_copy(rnd, off):
+        at = gslice(unit_at(rnd, off, xcol))
+        return remote(gown.at[at], xin.at[rnd, off], x_send.at[rnd, off], x_recv.at[rnd, off], (core, xnbr))
+
+    def y_copy(rnd, off):
+        at = gslice(unit_at(rnd, off, ycol))
+        return remote(gown.at[at], yin.at[rnd, off], y_send.at[rnd, off], y_recv.at[rnd, off], (core, ynbr))
+
+    def z_copy(rnd, off):
+        at = gslice(unit_at(rnd, off, col))
+        return remote(
+            gown.at[at], zin.at[rnd, off], z_send.at[rnd, off], z_recv.at[rnd, off], (core, plane(off) * 4 + col)
+        )
+
+    def add(at, other_ref):
+        gown[at] = (gown[at].astype(F32) + other_ref[...].astype(F32)).astype(BF)
+
+    def stage_zero(rnd, off):
+        for column in (dcol, xcol, ycol, col):
+            at = gslice(unit_at(rnd, off, column))
+            add(at, sib.at[at])
+        da_copy(rnd, off).start()
+        db_copy(rnd, off).start()
+
+    def stage_one(rnd, off):
+        da_copy(rnd, off).wait_recv()
+        add(ghalf(unit_at(rnd, off, xcol), 0), dain.at[rnd, off])
+        x_copy(rnd, off).start()
+        db_copy(rnd, off).wait_recv()
+        add(ghalf(unit_at(rnd, off, ycol), 1), dbin.at[rnd, off])
+        y_copy(rnd, off).start()
+
+    def stage_two(rnd, off):
+        x_copy(rnd, off).wait_recv()
+        y_copy(rnd, off).wait_recv()
+        at = gslice(unit_at(rnd, off, col))
+        gown[at] = (
+            gown[at].astype(F32) + xin[rnd, off].astype(F32) + yin[rnd, off].astype(F32)
+        ).astype(BF)
+
+    def a2a_copy(rnd, step):
+        dest = lax.rem(chip + step, CHIPS)
+        rng, til = unit_place(rnd * CHIPS + chip)
+        return remote(
+            expand.at[rnd, pl.ds(pl.multiple_of(dest * PAIR_ROWS, 16), PAIR_ROWS), :],
+            slot_ref.at[
+                pl.ds(pl.multiple_of(rng * PAIR_ROWS, 16), PAIR_ROWS),
+                pl.ds(pl.multiple_of(core * HALF + til * TILE, TILE), TILE),
+            ],
+            a2a_send.at[rnd, step], a2a_recv.at[rnd, step], (core, dest),
+        )
+
+    def stage_three(rnd):
+        for off in (1, 2, 3):
+            z_copy(rnd, off).wait_recv()
+        at = gslice(unit_at(rnd, 0, col))
+        total = gown[at].astype(F32)
+        for off in (1, 2, 3):
+            total = total + zin[rnd, off].astype(F32)
+        total = total.astype(BF)
+        for part in range(4):
+            rows = PACK_ROWS // 4
+            onehot = (
+                lax.broadcasted_iota(jnp.int32, (rows, RANGE_ROWS), 0) + part * rows
+                == idx_unit_ref[rnd : rnd + 1, :]
+            ).astype(F32).astype(BF)
+            expand[rnd, part * rows : (part + 1) * rows, :] = dotf(onehot, total).astype(BF)
+        for step in range(1, CHIPS):
+            a2a_copy(rnd, step).start()
+        rng, til = unit_place(rnd * CHIPS + chip)
+        slot_ref[
+            pl.ds(pl.multiple_of(rng * PAIR_ROWS, 16), PAIR_ROWS),
+            pl.ds(pl.multiple_of(core * HALF + til * TILE, TILE), TILE),
+        ] = expand[rnd, pl.ds(pl.multiple_of(chip * PAIR_ROWS, 16), PAIR_ROWS), :]
+
+    offsets = (1, 2, 3, 0)
+
+    def pump(p):
+        @pl.when(p < 8)
+        def _():
+            stage_zero(2 - p // 4, lax.rem(p % 4 + 1, 4))
+
+        @pl.when(jnp.logical_and(p >= 1, p < 9))
+        def _():
+            stage_one(2 - (p - 1) // 4, lax.rem((p - 1) % 4 + 1, 4))
+
+        @pl.when(jnp.logical_and(p >= 2, p < 10))
+        def _():
+            stage_two(2 - (p - 2) // 4, lax.rem((p - 2) % 4 + 1, 4))
+
+            @pl.when((p - 2) % 4 < 3)
+            def _():
+                z_copy(2 - (p - 2) // 4, (p - 2) % 4 + 1).start()
+
+    def p_copy(step, head):
+        seq, pair = step // 6, step % 6
+        return pltpu.make_async_copy(
+            p_hbm.at[seq * HEADS + pair * 2 + head], p_scr.at[step % 2, head], p_sem.at[step % 2, head]
+        )
+
+    rb_all = pltpu.make_async_copy(rb_hbm, gin_ref, r_sem)
+    rb_all.start()
+    for head in range(2):
+        p_copy(0, head).start()
+    diag[...] = jnp.zeros_like(diag)
+    for part in range(ntok // 128):
+        rows = slice(part * 128, (part + 1) * 128)
+        values = tokens_ref[rows, :].astype(F32)
+        inv_rms = lax.rsqrt(jnp.mean(values * values, axis=-1, keepdims=True) + EPS_NORM)
+        hid_t[:, rows] = (values * inv_rms * gains_ref[0:1, :]).astype(BF).T
+    lane_head = lax.broadcasted_iota(jnp.int32, (LEN, 128), 1) // HEAD_DIM
+
+    def attend_back(step, _):
+        seq, pair = step // 6, step % 6
+        rows = pl.ds(pl.multiple_of(seq * LEN, LEN), LEN)
+        lanes = pl.ds(pl.multiple_of(pair * 128, 128), 128)
+
+        @pl.when(step + 1 < 12)
+        def _():
+            for head in range(2):
+                p_copy(step + 1, head).start()
+
+        q_two, k_two, v_two, do_two = q_ref[rows, lanes], k_ref[rows, lanes], v_ref[rows, lanes], cb_ref[rows, lanes]
+        k_turn = k_two.T
+        inner = (do_two.astype(F32) * ctx_ref[rows, lanes].astype(F32)).T
+        dv_parts, dk_parts, dq_parts = [], [], []
+        for head in range(2):
+            p_copy(step, head).wait()
+            delta = jnp.sum(inner[head * HEAD_DIM : (head + 1) * HEAD_DIM], axis=0, keepdims=True)
+            v_one = jnp.where(lane_head == head, v_two, jnp.zeros_like(v_two))
+            for blk in range(4):
+                sub = slice(blk * 128, (blk + 1) * 128)
+                prob_back = dotf(v_one[sub], do_two, NT)
+                score = p_scr[step % 2, head, sub, :].astype(F32) * (prob_back - delta)
+                diag[pair * 2 + head, :, 384 - 128 * blk : 896 - 128 * blk] += score
+                ds_scr[head, sub, :] = score.astype(BF)
+            dv_parts.append(dotf(p_scr[step % 2, head], do_two))
+            dk_parts.append(dotf(ds_scr[head], q_two))
+            dq_parts.append(dotf(k_turn[head * HEAD_DIM : (head + 1) * HEAD_DIM], ds_scr[head]))
+        dv[rows, lanes] = jnp.where(lane_head == 0, dv_parts[0], dv_parts[1]).astype(BF)
+        dk[rows, lanes] = jnp.where(lane_head == 0, dk_parts[0], dk_parts[1]).astype(BF)
+        dq[rows, lanes] = jnp.concatenate(dq_parts, axis=0).T.astype(BF)
+        return 0
+
+    for rng in reversed(range(qkv_ranges, nrange)):
+        load_copy(rng).wait()
+        sib_wait(rng)
+
+    def step_both(step, _):
+        pump(step)
+        attend_back(step, 0)
+        return 0
+
+    lax.fori_loop(0, 12, step_both, 0)
+
+    w_all.wait()
+    for mat, grad in enumerate((dq, dk, dv)):
+        mat_rows = slice(mat * model, (mat + 1) * model)
+        for part in range(2):
+            value = dotf(hid_t[...], grad[:, part * HALF : (part + 1) * HALF]).astype(BF)
+
+            @pl.when(core == part)
+            def _():
+                gown[mat_rows, :] = value
+
+            @pl.when(core != part)
+            def _():
+                gsend[mat_rows, :] = value
+
+    for rng in range(qkv_ranges):
+        sib_copy(rng).start()
+
+    rb_all.wait()
+    tile = 256
+
+    def tail(i, gain):
+        rows = pl.ds(pl.multiple_of(i * tile, tile), tile)
+        u = (
+            dotf(dq[rows, :], weights[:model, :], NT)
+            + dotf(dk[rows, :], weights[model : 2 * model, :], NT)
+            + dotf(dv[rows, :], weights[2 * model :, :], NT)
+        )
+        value = tokens_ref[rows, :].astype(F32)
+        inv_rms = lax.rsqrt(jnp.mean(value * value, axis=-1, keepdims=True) + EPS_NORM)
+        gu = u * gains_ref[0:1, :]
+        normal = value * inv_rms
+        mean = jnp.mean(gu * normal, axis=-1, keepdims=True)
+        gin_ref[rows, :] += inv_rms * (gu - normal * mean)
+        return gain + jnp.sum((u * normal).reshape(tile // 8, 8, model), axis=0)
+
+    gain = lax.fori_loop(0, ntok // tile, tail, jnp.zeros((8, model), F32))
+
+    for rng in range(qkv_ranges):
+        sib_wait(rng)
+    stage_three(2)
+    stage_three(1)
+    for off in offsets:
+        stage_zero(0, off)
+    for off in offsets:
+        stage_one(0, off)
+
+    def unskew(h, _):
+        acc = jnp.concatenate([diag[h], jnp.zeros((128, 128), F32)], axis=1)
+        size = 64
+        while size >= 1:
+            acc = acc[:size] + pltpu.roll(acc[size:], 1024 - size, 1)
+            size //= 2
+        drow[pl.ds(h, 1), :] = acc
+        return 0
+
+    drow[...] = jnp.zeros_like(drow)
+    lax.fori_loop(0, HEADS, unskew, 0)
+    onehot = (lax.broadcasted_iota(jnp.int32, (128, 1024), 0) == bucket_ref[...]).astype(F32)
+    table = lax.dot_general(drow[...], onehot, NT, precision=HIGHEST, preferred_element_type=F32)
+    small[0, :, :model] = jnp.zeros((16, model), F32)
+    small[0, 0:1, :model] = jnp.sum(gain, axis=0, keepdims=True)
+    small[0, 1:2, :model] = jnp.sum(gain_two_ref[...], axis=0, keepdims=True)
+    small[0, :, model:] = table
+
+    for off in offsets:
+        stage_two(0, off)
+        if off:
+            z_copy(0, off).start()
+
+    def sm_copy(slot, src, dst, device):
+        return remote(small.at[src], small.at[dst], sm_send.at[slot], sm_recv.at[slot], device)
+
+    for slot, device in enumerate(((other, chip), (core, xnbr), (core, ynbr))):
+        cp = sm_copy(slot, 2 * slot, 2 * slot + 1, device)
+        cp.start()
+        cp.wait()
+        small[2 * slot + 2] = small[2 * slot] + small[2 * slot + 1]
+    for off in (1, 2, 3):
+        sm_copy(2 + off, 6, 7 + zpos, (core, plane(off) * 4 + col)).start()
+    small[7 + zpos] = small[6]
+
+    stage_three(0)
+
+    for off in (1, 2, 3):
+        sm_copy(2 + off, 6, 7 + zpos, (core, plane(off) * 4 + col)).wait()
+    small_ref[...] = small[7] + small[8] + small[9] + small[10]
+
+    for rnd in range(ROUNDS):
+        for step in range(1, CHIPS):
+            a2a_copy(rnd, step).wait_recv()
+    half = remote(
+        slot_ref.at[:, own_cols], slot_ref.at[:, own_cols], half_send, half_recv, (other, chip)
+    )
+    half.start()
+    for rng in range(nrange):
+        sib_copy(rng).wait_send()
+    for rnd in range(ROUNDS):
+        for step in range(1, CHIPS):
+            a2a_copy(rnd, step).wait_send()
+        for off in range(4):
+            x_copy(rnd, off).wait_send()
+            y_copy(rnd, off).wait_send()
+            da_copy(rnd, off).wait_send()
+            db_copy(rnd, off).wait_send()
+            if off:
+                z_copy(rnd, off).wait_send()
+    half.wait()
+
+
+def reduce_backward(
+    tokens, gains, q, k, v, ctx, cb, bucket_row, gain_two, idx_unit, rb, w_all, probs, grads
+):
+    ntok, model = tokens.shape
+    rows = w_all.shape[0]
+    dma = pltpu.SemaphoreType.DMA
+    unit_half = RANGE_ROWS // 2
+    return pl.pallas_call(
+        reduce_kernel,
+        name="reduce_backward",
+        out_shape=(
+            jax.ShapeDtypeStruct((ntok, model), F32),
+            jax.ShapeDtypeStruct((PACK_ROWS, model), BF),
+            jax.ShapeDtypeStruct((16, model + 128), F32),
+        ),
+        in_specs=[VM] * 10 + [ANY] * 4,
+        out_specs=(VM, VM, VM),
+        scratch_shapes=[
+            pltpu.VMEM((3 * model, model), BF),
+            pltpu.VMEM((rows, HALF), BF),
+            pltpu.VMEM((3 * model, HALF), BF),
+            pltpu.VMEM((rows, HALF), BF),
+            pltpu.VMEM((ROUNDS, 4, RANGE_ROWS, TILE), BF),
+            pltpu.VMEM((ROUNDS, 4, RANGE_ROWS, TILE), BF),
+            pltpu.VMEM((ROUNDS, 4, unit_half, TILE), BF),
+            pltpu.VMEM((ROUNDS, 4, unit_half, TILE), BF),
+            pltpu.VMEM((ROUNDS, 4, RANGE_ROWS, TILE), BF),
+            pltpu.VMEM((ROUNDS, PACK_ROWS, TILE), BF),
+            pltpu.VMEM((model, ntok), BF),
+            pltpu.VMEM((ntok, model), BF),
+            pltpu.VMEM((ntok, model), BF),
+            pltpu.VMEM((ntok, model), BF),
+            pltpu.VMEM((HEADS, 128, 896), F32),
+            pltpu.VMEM((16, 1024), F32),
+            pltpu.VMEM((2, 2, LEN, LEN), BF),
+            pltpu.VMEM((2, LEN, LEN), BF),
+            pltpu.VMEM((11, 16, model + 128), F32),
+            dma, dma((CHIPS,)), dma((2, 2)), dma, dma((CHIPS,)), dma((CHIPS,)),
+            dma((ROUNDS, 4)), dma((ROUNDS, 4)), dma((ROUNDS, 4)), dma((ROUNDS, 4)),
+            dma((ROUNDS, 4)), dma((ROUNDS, 4)), dma((ROUNDS, 4)), dma((ROUNDS, 4)),
+            dma((ROUNDS, 4)), dma((ROUNDS, 4)),
+            dma((ROUNDS, CHIPS)), dma((ROUNDS, CHIPS)), dma, dma,
+            dma((6,)), dma((6,)),
+        ],
+        compiler_params=pltpu.CompilerParams(
+            collective_id=1, has_side_effects=True, vmem_limit_bytes=62 * 2**20
+        ),
+    )(tokens, gains, q, k, v, ctx, cb, bucket_row, gain_two, idx_unit, rb, w_all, probs, grads)
+
+
 BETA_ONE = 0.5
 BETA_TWO = 0.75
 LEARN_RATE = 0.06
 SMALL_RATE = 0.4
 WEIGHT_DECAY = 0.01
 EPS_ADAM = 1e-08
-NEG_FILL = -1e30
-HIGHEST = lax.Precision.HIGHEST
+OPT_STEP = 3
+
+
+def adamw(weight, gradient, first_in, second, rate):
+    first_out = BETA_ONE * first_in + (1.0 - BETA_ONE) * gradient
+    second_out = BETA_TWO * second + (1.0 - BETA_TWO) * gradient * gradient
+    fix_first = 1.0 - BETA_ONE**OPT_STEP
+    fix_second = 1.0 - BETA_TWO**OPT_STEP
+    update = first_out / fix_first / (jnp.sqrt(second_out / fix_second) + EPS_ADAM)
+    return (first_out, second_out, weight - rate * (update + WEIGHT_DECAY * weight))
+
+
+def adam_kernel(idx_ref, packed_ref, master_ref, first_ref, second_ref, grad_ref, fnew_ref, snew_ref, mnew_ref, copy_ref):
+    rows = master_ref.shape[0]
+    onehot = (
+        lax.broadcasted_iota(jnp.int32, (rows, PACK_ROWS), 0) + pl.program_id(0) * rows == idx_ref[...]
+    ).astype(F32).astype(BF)
+    grad = dotf(onehot, packed_ref[...])
+    first_new, second_new, master_new = adamw(
+        master_ref[...], grad, first_ref[...], second_ref[...], LEARN_RATE
+    )
+    grad_ref[...] = grad
+    fnew_ref[...] = first_new
+    snew_ref[...] = second_new
+    mnew_ref[...] = master_new
+    copy_ref[...] = master_new.astype(BF)
+
+
+def adam_slots(idx_row, packed, master, first, second):
+    rows, model = master.shape
+    tile = 144
+    blk = pl.BlockSpec((tile, model), lambda i: (i, 0))
+    full = lambda a: pl.BlockSpec(a.shape, lambda i: (0, 0))
+    wide = jax.ShapeDtypeStruct((rows, model), F32)
+    return pl.pallas_call(
+        adam_kernel,
+        name="adam_slots",
+        grid=(rows // tile,),
+        out_shape=(wide, wide, wide, wide, jax.ShapeDtypeStruct((rows, model), BF)),
+        in_specs=[full(idx_row), full(packed), blk, blk, blk],
+        out_specs=(blk,) * 5,
+        compiler_params=pltpu.CompilerParams(vmem_limit_bytes=48 * 2**20),
+    )(idx_row, packed, master, first, second)
+
+
+def fast_body(
+    tokens, cotangent, master_slots, first_slots, second_slots, norm_gains, gains_first, gains_second,
+    bias_table, table_first, table_second, bucket_ids, valid_len, task_sizes, owner_list,
+):
+    chip = lax.axis_index("fsdp")
+    model = tokens.shape[1]
+    pack, unit = slot_tables(owner_list, chip)
+    rel = rel_values(bias_table, bucket_ids)
+    turned = jnp.concatenate([bucket_ids[::-1], jnp.full((1,), -1, jnp.int32)])
+    bucket_row = jnp.concatenate([turned[127:], turned[:127]])[None, :]
+    seq_weight = sequence_weights(valid_len.shape[0], task_sizes)
+    w_all, q, k, v, ctx, probs = gather_forward(
+        master_slots, pack[:, None], unit[:, :, None], tokens, norm_gains, rel, valid_len
+    )
+    block_out, rb, cb, gain_two, grads = ffn_pass(tokens, cotangent, ctx, norm_gains, seq_weight, w_all)
+    grad_input, packed, small = reduce_backward(
+        tokens, norm_gains, q, k, v, ctx, cb, bucket_row, gain_two, unit, rb, w_all, probs, grads
+    )
+    grad_gains = small[:2, :model]
+    grad_table = small[: bias_table.shape[1], model : model + bias_table.shape[0]].T
+    grad_slots, first_new, second_new, master_new, master_copy = adam_slots(
+        pack[None, :], packed, master_slots, first_slots, second_slots
+    )
+    gains_first_new, gains_second_new, gains_new = adamw(
+        norm_gains, grad_gains, gains_first, gains_second, SMALL_RATE
+    )
+    table_first_new, table_second_new, table_new = adamw(
+        bias_table, grad_table, table_first, table_second, SMALL_RATE
+    )
+    return (
+        block_out, grad_input, grad_slots, grad_gains, grad_table, first_new, second_new, master_new, master_copy,
+        gains_first_new, gains_second_new, gains_new, table_first_new, table_second_new, table_new,
+    )
+
+
+def sequence_weights(seq_dev, task_sizes):
+    first_seq = (lax.axis_index("dp") * lax.axis_size("fsdp") + lax.axis_index("fsdp")) * seq_dev
+    seq_ids = first_seq + jnp.arange(seq_dev, dtype=jnp.int32)
+    task_ends = jnp.cumsum(task_sizes)
+    task_count = task_sizes.shape[0]
+    task_of = jnp.sum((task_ends[None, :] <= seq_ids[:, None]).astype(jnp.int32), axis=1)
+    size_of = jnp.sum(
+        jnp.where(
+            task_of[:, None] == jnp.arange(task_count, dtype=jnp.int32)[None, :], task_sizes[None, :], 0
+        ),
+        axis=1,
+    )
+    total = seq_dev * lax.axis_size("dp") * lax.axis_size("fsdp")
+    return jnp.float32(total) / (jnp.float32(task_count) * size_of.astype(F32))
 
 
 def product(left_side, right_side):
@@ -97,7 +1155,7 @@
     return jnp.where(live, scores, NEG_FILL)
 
 
-def adamw(weight, gradient, first_in, second, step_value, rate):
+def adamw_step(weight, gradient, first_in, second, step_value, rate):
     first_out = BETA_ONE * first_in + (1.0 - BETA_ONE) * gradient
     second_out = BETA_TWO * second + (1.0 - BETA_TWO) * gradient * gradient
     fix_first = 1.0 - jnp.power(jnp.float32(BETA_ONE), step_value)
@@ -106,7 +1164,7 @@
     return (first_out, second_out, weight - rate * (update + WEIGHT_DECAY * weight))
 
 
-def body(
+def plain_body(
     tokens,
     cotangent,
     master_slots,
@@ -270,13 +1328,13 @@
     grad_slots = lax.psum(owned_grads, "dp")
     grad_gains, grad_table = lax.psum((jnp.stack([gain_one, gain_two]), table_grad), ("dp", "fsdp"))
     step_value = jnp.float32(OPT_STEP)
-    first_new, second_new, master_new = adamw(
+    first_new, second_new, master_new = adamw_step(
         master_slots, grad_slots, first_slots, second_slots, step_value, LEARN_RATE
     )
-    gains_first_new, gains_second_new, gains_new = adamw(
+    gains_first_new, gains_second_new, gains_new = adamw_step(
         norm_gains, grad_gains, gains_first, gains_second, step_value, SMALL_RATE
     )
-    table_first_new, table_second_new, table_new = adamw(
+    table_first_new, table_second_new, table_new = adamw_step(
         bias_table, grad_table, table_first, table_second, step_value, SMALL_RATE
     )
     return (
@@ -333,4 +1391,7 @@
         P(),
         P(),
     )
-    return jax.shard_map(body, mesh=mesh, in_specs=in_specs, out_specs=out_specs, check_vma=False)
+    fast = dict(mesh.shape) == {"dp": 2, "fsdp": CHIPS}
+    body = fast_body if fast else plain_body
+    return jax.shard_map(
+        body, mesh=mesh, in_specs=in_specs, out_specs=out_specs, check_vma=False)

time: 1790 us -> 365 us (0.20)
  waiting for transfers between devices: 826 us -> 0 us
  local copies, waits for them, and re-layouts: 594 us -> 11.6 us
  Pallas kernels: 0 us -> 331 us
  matrix products: 187 us -> 1.16 us
  other arithmetic: 107 us -> 9.52 us
  blocking collectives: 39.7 us -> 0 us
    reduce_scatter x1 -> x0, waiting for transfers between devices: 773 us -> none  [body(): lax.psum_scatter(slotted, 'fsdp', scatter_dimension=0, tiled=True)]
    pallas_call x0 -> x4, Pallas kernels: none -> 331 us  [the longest x1 136 us: reduce_backward(): pl.pallas_call(reduce_kernel, name='reduce_backward', out_shape=(jax.Shap...]
    rev x2 -> x0, local copies, waits for them, and re-layouts: 197 us -> none  [expand_bias(): tiled_rows.reshape(reverse.shape[0], length, 2 * length)[:, :, :length]]
    dot_general x34 -> x1, matrix products: 187 us -> 1.16 us  [rel_values(): rel = jnp.dot(onehot, bias_table, precision=HIGHEST)[::-1].T]
    unnamed x112 -> x26, local copies, waits for them, and re-layouts: 113 us -> 6.7 us
    gather x2 -> x0, local copies, waits for them, and re-layouts: 73.3 us -> none  [the longest x1 56.3 us: body(): grad_rows.reshape(-1, BROWS, model_width)[source]]
    another operation x7 -> x1, local copies, waits for them, and re-layouts: 57.1 us -> 0.74 us  [the longest x2 51.8 us: expand_bias(): tiled_rows = jnp.tile(reverse, (1, length + 1))[:, :2 * length * length]]
    reshape x7 -> x1, local copies, waits for them, and re-layouts: 55.6 us -> 0.78 us  [slot_tables(): owners = owner_list.reshape(CHIPS, RANGE_BLOCKS)]
  transfers between devices with their start and end apart: 3 -> 0, of which waited for: 2 -> 0; matrix products, arithmetic and copies ran while one was open for 28% -> 0% of each run, Pallas kernels for 0% -> 0%
where the time goes in v1:
time: 365 us; the launch traced here: 360 us
  Pallas kernels  331 us (91%)
  local copies, waits for them, and re-layouts  11.6 us (3%)
  other arithmetic  9.52 us (3%)
  between operations  6.88 us (2%)
    pallas_call x1, Pallas kernels, reduce_backward(): pl.pallas_call(reduce_kernel, name='reduce_backward', out_shape=(jax.Shap...  136 us
    pallas_call x1, Pallas kernels, gather_forward(): pl.pallas_call(gather_kernel, name='gather_forward', out_shape=(jax.Shape...  134 us
    pallas_call x1, Pallas kernels, ffn_pass(): pl.pallas_call(ffn_kernel, name='ffn_pass', out_shape=(jax.ShapeDtypeStru...  49 us
    pallas_call x1, Pallas kernels, adam_slots(): pl.pallas_call(adam_kernel, name='adam_slots', grid=(rows // tile,), out_...  11.9 us

profile of v1, /device:TPU:0, one launch (start us, length us, event | category | flops | bytes accessed | tf_op | source)
XLA Modules:
  0.0 360.3 jit_solution(7974139442863737771)
XLA Ops:
  0.7 0.7 slice.36
  1.4 0.1 slice.37
  1.5 0.6 fusion.8
  7.9 0.8 reverse.2
  8.6 0.1 slice.44
  8.7 0.1 pad_add_fusion
  8.8 0.1 slice.35
  8.9 0.7 pad_add_fusion.1
  9.5 0.8 reshape.266
  10.3 0.1 convert_reduce_fusion.1
  10.4 0.1 select_reduce_fusion
  10.6 0.1 iota_compare_fusion.5
  10.7 0.1 add_multiply_fusion
  10.7 0.2 convert_reduce_fusion
  11.0 0.7 copy.40
  11.7 0.1 reduce-window.8
  11.8 0.1 reduce
  11.9 0.2 fusion.4
  12.1 0.8 fusion.5
  12.9 0.5 multiply_divide_fusion.weight_ref
  13.5 0.1 add.168
  13.6 1.2 fusion
  14.7 0.6 reverse.1
  15.3 0.1 slice_bitcast_fusion.2
  15.4 0.1 pad_slice_fusion
  15.5 0.7 select_maximum_fusion.rel_ref
  16.2 0.1 add.165
  16.3 0.1 add.174
  16.4 0.6 broadcast_add_fusion.1.idx_unit_ref
  17.0 0.1 add_select_fusion
  17.2 0.1 select_n.54.idx_ref
  17.3 1.1 select_n.55.idx_pack_ref
  18.3 0.3 add.187
  18.6 1.1 broadcast_add_fusion.idx_unit_ref
  19.7 134.2 %gather_forward.1 = (bf16[9216,768]{1,0:T(8,128)(2,1)}, bf16[1024,768]{1,0:T(8,128)(2,1)}, bf16[1024,768]{1,0:T(8,128)(2,1)}, bf16[1024,768]{1,0:T(8,128)(2,1)},...) custom-call(f32[1152,768]{1,0:T(8,128)} %master_ref.3, s32[1280,1]{1,0:T(8,128)} %select_n.55.idx_pack_ref, ...), custom_call_target="tpu_custom_call" | custom-call | tf_op jit(solution)/shard_map/gather_forward/pallas_call | solution.py:362
  153.9 49.0 %ffn_pass.1 = (bf16[1024,768]{1,0:T(8,128)(2,1)}, f32[1024,768]{1,0:T(8,128)}, bf16[1024,768]{1,0:T(8,128)(2,1)}, f32[8,768]{1,0:T(8,128)}, bf16[9216,768]{1,0:T(8,128)(2,1)}) custom-call(bf16[1024,768]{1,0:T(8,128)(2,1)} %tokens_ref.5, bf16[1024,768]{1,0:T(8,128)(2,1)} %cot_ref.1, bf16[1024,768]{1,0:T(8,128)(2,1)} %get-tuple-element.34.ctx_ref, ...), custom_call_target="tpu_custom_call" | custom-call | tf_op jit(solution)/shard_map/ffn_pass/pallas_call | solution.py:561
  202.9 0.0 copy-start.3
  202.9 0.0 copy-start.10
  202.9 0.0 copy-start.4
  202.9 136.1 %reduce_backward.1 = (f32[1024,768]{1,0:T(8,128)}, bf16[1280,768]{1,0:T(8,128)(2,1)}, f32[16,896]{1,0:T(8,128)}) custom-call(bf16[1024,768]{1,0:T(8,128)(2,1)} %tokens_ref.5, f32[2,768]{1,0:T(2,128)} %gains_ref.5, bf16[1024,768]{1,0:T(8,128)(2,1)} %get-tuple-element.37.q_ref, bf16[1024,768]{1,0:T(8,128)(2,1)} %get-tuple-element.38.k_ref, ...), custom_call_target="tpu_custom_call" | custom-call | tf_op jit(solution)/shard_map/reduce_backward/pallas_call | solution.py:937
  339.1 1.4 multiply_subtract_fusion.1
  340.5 1.3 multiply_subtract_fusion
  341.8 0.6 broadcast_multiply_fusion.1
  342.4 0.6 broadcast_multiply_fusion
  343.0 2.0 copy-done
  345.0 1.5 copy-done.1
  346.6 11.9 %adam_slots.1 = (f32[1152,768]{1,0:T(8,128)}, f32[1152,768]{1,0:T(8,128)}, f32[1152,768]{1,0:T(8,128)}, f32[1152,768]{1,0:T(8,128)}, bf16[1152,768]{1,0:T(8,128)(2,1)}) custom-call(s32[1,1280]{1,0:T(1,128)S(1)} %select_n.54.idx_ref, bf16[1280,768]{1,0:T(8,128)(2,1)S(1)} %copy-done.1, f32[1152,768]{1,0:T(8,128)S(1)} %copy-done, f32[1152,768]{1,0:T(8,128)} %first_ref.1, ...), custom_call_target="tpu_custom_call" | custom-call | tf_op jit(solution)/shard_map/adam_slots/pallas_call | solution.py:1020
  358.4 1.7 copy.42
  (25 shorter events, 0.1 us)
Async XLA Ops:
  202.9 136.2 %copy-start.3 = (f32[2,768]{1,0:T(2,128)S(1)}, f32[2,768]{1,0:T(2,128)}, u32[]{:S(2)}) copy-start(f32[2,768]{1,0:T(2,128)} %gains_ref.5) | copy-start | bytes 18436
  202.9 136.2 %copy-start.6 = (f32[2,768]{1,0:T(2,128)S(1)}, f32[2,768]{1,0:T(2,128)}, u32[]{:S(2)}) copy-start(f32[2,768]{1,0:T(2,128)} %param.21) | copy-start | bytes 18436
  202.9 136.2 %copy-start.10 = (f32[2,768]{1,0:T(2,128)S(1)}, f32[2,768]{1,0:T(2,128)}, u32[]{:S(2)}) copy-start(f32[2,768]{1,0:T(2,128)} %param.22) | copy-start | bytes 18436
  202.9 137.6 %copy-start.4 = (f32[32,12]{0,1:T(8,128)S(1)}, f32[32,12]{0,1:T(8,128)}, u32[]{:S(2)}) copy-start(f32[32,12]{0,1:T(8,128)} %param.24) | copy-start | bytes 4612
  202.9 137.6 %copy-start.8 = (f32[32,12]{0,1:T(8,128)S(1)}, f32[32,12]{0,1:T(8,128)}, u32[]{:S(2)}) copy-start(f32[32,12]{0,1:T(8,128)} %param.23) | copy-start | bytes 4612
  202.9 137.5 %copy-start.9 = (f32[32,12]{0,1:T(8,128)S(1)}, f32[32,12]{0,1:T(8,128)}, u32[]{:S(2)}) copy-start(f32[32,12]{0,1:T(8,128)} %param.25) | copy-start | bytes 4612
  340.5 18.0 %copy-start.7 = (f32[2,768]{1,0:T(2,128)}, f32[2,768]{1,0:T(2,128)S(1)}, u32[]{:S(2)}) copy-start(f32[2,768]{1,0:T(2,128)S(1)} %get-tuple-element.83) | copy-start | bytes 18436
  341.8 16.6 %copy-start.5 = (f32[32,12]{0,1:T(8,128)}, f32[32,12]{0,1:T(8,128)S(1)}, u32[]{:S(2)}) copy-start(f32[32,12]{0,1:T(8,128)S(1)} %get-tuple-element.84) | copy-start | bytes 4612
  343.0 2.0 copy-start
  345.0 1.5 copy-start.1
  346.6 11.9 %copy-start.2 = (f32[1024,768]{1,0:T(8,128)S(1)}, f32[1024,768]{1,0:T(8,128)}, u32[]{:S(2)}) copy-start(f32[1024,768]{1,0:T(8,128)} %get-tuple-element.81) | copy-start | bytes 9437188
